TPU v7x, 512 devices: a whole 4x4x16 slice. The times are simulated.
512 devices in a mesh: ctx: 32 (over z, core), tp: 4 (over x), dp: 4 (over y).
Axes of the slice: x: 4, y: 4, z: 16, core: 2. Of those that a mesh axis runs over, the one named last changes fastest.
Arguments:
- attention_out: bfloat16 [8192, 4096], P('ctx', ('tp', 'dp')), may hold values from -6 to 6
- output_weight: bfloat16 [4096, 2048], P(('tp', 'dp')), may hold values from -0.09375 to 0.09375
- residual: bfloat16 [8192, 2048], P(('ctx', 'tp')), may hold values from -6 to 6
- norm_gain: float32 [2048], replicated, may hold values from 0.25 to 1.75
- routed_experts: int32 [8192, 8], P(('ctx', 'tp')), may hold values from 0 to 127, as said below
- route_weights: float32 [8192, 8], P(('ctx', 'tp')), may hold values from 0.05 to 1
- gate_weight: bfloat16 [128, 1024, 2048], P(('ctx', 'tp'), 'dp'), may hold values from -0.125 to 0.125
- up_weight: bfloat16 [128, 1024, 2048], P(('ctx', 'tp'), 'dp'), may hold values from -0.125 to 0.125
- down_weight: bfloat16 [128, 1024, 2048], P(('ctx', 'tp'), 'dp'), may hold values from -0.75 to 0.75
Outputs:
- layer_out: bfloat16 [8192, 2048], P(('ctx', 'tp', 'dp'))
Inputs may be any that keep to these rules, and one draw needn't show every extreme that they name: `routed_experts`: each row names 8 different experts. In each aligned block of 64 rows no expert is named by more than 8 rows, and one expert, the same for all blocks, is named by exactly 8 rows in every block.
All inputs are finite; a program needn't handle non-finite values.
Results may differ from a plain program's by a relative error of at most 0.009.
Values may be sent and summed in bfloat16 or wider, within the bound.
A program may use at most 64 MiB of HBM per device.

v0:
```python
import jax
import jax.numpy as jnp
from jax import lax
from jax.sharding import PartitionSpec as P

EPSILON = 1e-06


def split_up(value, dim, devices):
    lengths = value.shape
    pieces = value.reshape(*lengths[:dim], devices, lengths[dim] // devices, *lengths[dim + 1 :])
    return jnp.moveaxis(pieces, dim, 0)


def sum_at_owner(value, axis, dim):
    pieces = split_up(value, dim, lax.axis_size(axis))
    arrived = lax.all_to_all(pieces, axis, split_axis=0, concat_axis=0, tiled=True)
    return arrived.sum(axis=0)


def sent_to_all(value, axis):
    devices = lax.axis_size(axis)
    return lax.all_to_all(
        jnp.broadcast_to(value[None], (devices, *value.shape)), axis, 0, 0, tiled=True
    )


def laid_out(pieces, dim):
    pieces = jnp.moveaxis(pieces, 0, dim)
    lengths = pieces.shape
    return pieces.reshape(*lengths[:dim], lengths[dim] * lengths[dim + 1], *lengths[dim + 2 :])


def gathered_copies(value, axis, dim):
    pieces = sent_to_all(value, axis)
    return laid_out(pieces, dim)


def summed_on_arrival(value, axis, dim):
    devices = lax.axis_size(axis)
    pieces = lax.all_to_all(split_up(value, dim, devices), axis, 0, 0, tiled=True)
    return jnp.sum(pieces.astype(jnp.float32), axis=0)


def on_device(
    attention_out,
    output_weight,
    residual,
    norm_gain,
    routed_experts,
    route_weights,
    gate_weight,
    up_weight,
    down_weight,
):
    row_count, model_width = residual.shape
    top_count = routed_experts.shape[1]
    replicas = lax.axis_size("dp")
    quarter = row_count // replicas
    replica = lax.axis_index("dp")
    context_count = lax.axis_size("ctx")
    tensor_count = lax.axis_size("tp")
    experts = context_count * tensor_count
    capacity = min(row_count, 2 * row_count * top_count // experts)
    summed = sum_at_owner(
        jnp.dot(attention_out, output_weight, preferred_element_type=jnp.float32), ("tp", "dp"), 0
    )
    own_residual = lax.dynamic_slice_in_dim(residual, replica * quarter, quarter, 0)
    own_state = own_residual.astype(jnp.float32) + summed
    square = jnp.mean(own_state * own_state, axis=-1, keepdims=True)
    normed = gathered_copies(
        (own_state * lax.rsqrt(square + EPSILON) * norm_gain).astype(jnp.bfloat16), "dp", 0
    )
    flat_ids = routed_experts.reshape(-1)
    copies = flat_ids.shape[0]
    after_mask = lax.broadcasted_iota(jnp.int32, (copies, copies), 0) > lax.broadcasted_iota(
        jnp.int32, (copies, copies), 1
    )
    before = jnp.sum(
        ((flat_ids[:, None] == flat_ids[None, :]) & after_mask).astype(jnp.int32), axis=1
    )
    slot_index = flat_ids * capacity + before
    source_rows = lax.broadcasted_iota(jnp.int32, (copies,), 0) // top_count
    outgoing = (
        jnp.zeros((experts * capacity, model_width), jnp.bfloat16)
        .at[slot_index]
        .set(normed[source_rows])
    )
    outgoing = outgoing.reshape(experts, capacity, model_width)
    gate_matrix = gate_weight[0]
    up_matrix = up_weight[0]
    down_matrix = down_weight[0]
    arrived = lax.all_to_all(outgoing, ("ctx", "tp"), split_axis=0, concat_axis=0, tiled=True)
    flat_rows = arrived.reshape(-1, model_width)
    gate_act = lax.dot_general(
        flat_rows, gate_matrix, (((1,), (1,)), ((), ())), preferred_element_type=jnp.float32
    )
    up_act = lax.dot_general(
        flat_rows, up_matrix, (((1,), (1,)), ((), ())), preferred_element_type=jnp.float32
    )
    hidden = (jax.nn.silu(gate_act) * up_act).astype(jnp.bfloat16)
    result = jnp.dot(hidden, down_matrix, preferred_element_type=jnp.float32)
    gathered_back = lax.all_to_all(
        result.reshape(arrived.shape[0], arrived.shape[1], model_width).astype(jnp.bfloat16),
        ("ctx", "tp"),
        split_axis=0,
        concat_axis=0,
        tiled=True,
    ).astype(jnp.float32)
    returned_flat = gathered_back.reshape(experts * capacity, model_width)
    copy_outputs = returned_flat[slot_index].reshape(row_count, top_count, model_width)
    route_probs = route_weights / jnp.sum(route_weights, axis=1, keepdims=True)
    mixed = jnp.sum(copy_outputs * route_probs[:, :, None], axis=1)
    routed = summed_on_arrival(mixed.astype(jnp.bfloat16), "dp", 0)
    return (own_state + routed).astype(jnp.bfloat16)


def solution(mesh):
    in_specs = (
        P("ctx", ("tp", "dp")),
        P(("tp", "dp"), None),
        P(("ctx", "tp"), None),
        P(),
        P(("ctx", "tp"), None),
        P(("ctx", "tp"), None),
        P(("ctx", "tp"), "dp", None),
        P(("ctx", "tp"), "dp", None),
        P(("ctx", "tp"), "dp", None),
    )
    out_specs = P(("ctx", "tp", "dp"), None)
    return jax.shard_map(
        on_device, mesh=mesh, in_specs=in_specs, out_specs=out_specs, check_vma=False
    )
```

profile of v0, /device:TPU:1, one launch (start us, length us, event | category | flops | bytes accessed | tf_op | source)
XLA Modules:
  0.0 504.3 jit_solution(17658465208792514045)
XLA Ops:
  0.0 0.0 copy-start
  0.0 0.0 copy-start.2
  0.0 0.0 copy-start.1
  0.0 3.2 fusion.22
  3.2 0.0 copy-start.4
  3.2 7.7 %all-to-all-start = ((f32[16,16,2048]{2,1,0:T(8,128)}), f32[16,16,2048]{2,1,0:T(8,128)S(1)}, u32[]{:S(2)}, u32[]{:S(2)}) async-start(f32[16,16,2048]{2,1,0:T(8,128)} %bitcast.40), calls=%async_computation | async-start | bytes 4194304 | tf_op jit(solution)/shard_map/all_to_all | solution.py:17
  10.9 0.0 copy-done.2
  10.9 0.1 copy.23
  11.0 0.1 copy.22
  11.1 0.1 mul.56
  11.2 0.1 eq.15
  11.3 0.6 pad_clamp_fusion.1
  11.9 0.2 convert_reduce_fusion
  12.2 24.1 %all-to-all-done = f32[16,16,2048]{2,1,0:T(8,128)S(1)} async-done(((f32[16,16,2048]{2,1,0:T(8,128)}), f32[16,16,2048]{2,1,0:T(8,128)S(1)}, u32[]{:S(2)}, u32[]{:S(2)}) %all-to-all-start) | async-done | bytes 2097184 | tf_op jit(solution)/shard_map/all_to_all | solution.py:17
  36.2 0.1 reduce_sum.56
  36.3 0.0 copy-done.1
  36.4 0.1 multiply_reduce_fusion
  36.5 0.0 copy-done.4
  36.5 0.1 multiply_convert_fusion
  36.6 0.7 broadcast_in_dim.5
  37.3 3.4 all-to-all-start.1
  40.7 5.5 %all-to-all-done.1 = bf16[4,16,2048]{2,1,0:T(8,128)(2,1)S(1)} async-done(((bf16[4,16,2048]{2,1,0:T(8,128)(2,1)}), bf16[4,16,2048]{2,1,0:T(8,128)(2,1)S(1)}, u32[]{:S(2)}, u32[]{:S(2)}) %all-to-all-start.1) | async-done | bytes 262176 | tf_op jit(solution)/shard_map/all_to_all | solution.py:23
  46.2 12.9 %scatter_custom_fusion = bf16[1024,2048]{1,0:T(8,128)(2,1)} fusion(s32[512]{0:T(512)S(1)} %bitcast.43, bf16[64,2048]{1,0:T(8,128)(2,1)S(1)} %bitcast.42, s32[1024]{0:T(1024)} %pad_clamp_fusion.1, bf16[]{:T(256)} %constant.35.clone.1), kind=kCustom, calls=%fused_computation.11 | custom fusion | bytes 4194816 | tf_op jit(solution)/shard_map/scatter | solution.py:87
  59.2 0.0 copy-start.5
  59.2 211.3 %all_to_all.25 = bf16[128,8,2048]{2,1,0:T(8,128)(2,1)S(1)} all-to-all(bf16[128,8,2048]{2,1,0:T(8,128)(2,1)} %bitcast.39), channel_id=1, replica_groups=mesh['ctx'=32,'tp'=4,'dp'=4] {'ctx','tp'}, dimensions={0} | all-to-all | bytes 8388608 | tf_op jit(solution)/shard_map/all_to_all | solution.py:93
  270.5 0.0 copy-done.5
  270.5 0.0 copy-start.6
  270.5 1.3 fusion.3
  271.8 0.0 copy-done.6
  271.8 1.4 fusion.14
  273.2 0.0 copy-done
  273.2 1.3 convolution_convert_fusion
  274.5 4.2 copy.25
  278.7 0.0 copy-start.3
  278.7 10.7 %all-to-all-start.3 = ((bf16[128,8,2048]{2,1,0:T(8,128)(2,1)}), bf16[128,8,2048]{2,1,0:T(8,128)(2,1)}, u32[]{:S(2)}, u32[]{:S(2)}) async-start(bf16[128,8,2048]{2,1,0:T(8,128)(2,1)} %copy.25), calls=%async_computation.3 | async-start | bytes 8388608 | tf_op jit(solution)/shard_map/all_to_all | solution.py:103
  289.4 0.0 copy-done.3
  289.5 0.1 copy.26
  289.6 186.6 %all-to-all-done.3 = bf16[128,8,2048]{2,1,0:T(8,128)(2,1)} async-done(((bf16[128,8,2048]{2,1,0:T(8,128)(2,1)}), bf16[128,8,2048]{2,1,0:T(8,128)(2,1)}, u32[]{:S(2)}, u32[]{:S(2)}) %all-to-all-start.3) | async-done | bytes 4194336 | tf_op jit(solution)/shard_map/all_to_all | solution.py:103
  476.2 6.5 %bitcast_convert_fusion = f32[1024,2048]{1,0:T(8,128)} fusion(bf16[128,8,2048]{2,1,0:T(8,128)(2,1)} %all-to-all-done.3), kind=kLoop, calls=%fused_computation.3 | loop fusion | flops 2097152 | bytes 12582912 | tf_op jit(solution)/shard_map/reshape | solution.py:110
  482.7 8.8 %gather_fusion = f32[512,2048]{1,0:T(8,128)} fusion(f32[1024,2048]{1,0:T(8,128)} %bitcast_convert_fusion, s32[1024]{0:T(1024)S(1)} %pad_clamp_fusion), kind=kCustom, calls=%fused_computation.1 | custom fusion | bytes 8390656 | tf_op jit(solution)/shard_map/gather | solution.py:111
  491.4 3.7 fusion
  495.1 8.5 %all_to_all.26 = bf16[4,16,2048]{2,1,0:T(8,128)(2,1)S(1)} all-to-all(bf16[4,16,2048]{2,1,0:T(8,128)(2,1)S(1)} %bitcast.41), channel_id=1, replica_groups=mesh['ctx'=32,'tp'=4,'dp'=4] {'dp'}, dimensions={0} | all-to-all | bytes 524288 | tf_op jit(solution)/shard_map/all_to_all | solution.py:41
  503.6 0.7 add_convert_fusion
  (8 shorter events, 0.1 us)
Async XLA Ops:
  0.0 273.2 %copy-start = (bf16[1,256,2048]{2,1,0:T(8,128)(2,1)S(1)}, bf16[1,256,2048]{2,1,0:T(8,128)(2,1)}, u32[]{:S(2)}) copy-start(bf16[1,256,2048]{2,1,0:T(8,128)(2,1)} %param.17) | copy-start | bytes 3145732
  0.0 10.9 %copy-start.2 = (s32[64,8]{0,1:T(8,128)S(1)}, s32[64,8]{0,1:T(8,128)}, u32[]{:S(2)}) copy-start(s32[64,8]{0,1:T(8,128)} %param.13) | copy-start | bytes 6148
  0.0 36.3 %copy-start.1 = (bf16[64,2048]{1,0:T(8,128)(2,1)S(1)}, bf16[64,2048]{1,0:T(8,128)(2,1)}, u32[]{:S(2)}) copy-start(bf16[64,2048]{1,0:T(8,128)(2,1)} %param.11) | copy-start | bytes 786436
  3.2 33.3 %copy-start.4 = (f32[2048]{0:T(1024)S(1)}, f32[2048]{0:T(1024)}, u32[]{:S(2)}) copy-start(f32[2048]{0:T(1024)} %param.12) | copy-start | bytes 24580
  3.2 33.0 %all-to-all-start = ((f32[16,16,2048]{2,1,0:T(8,128)}), f32[16,16,2048]{2,1,0:T(8,128)S(1)}, u32[]{:S(2)}, u32[]{:S(2)}) async-start(f32[16,16,2048]{2,1,0:T(8,128)} %bitcast.40), calls=%async_computation | async-start | bytes 4194304 | tf_op jit(solution)/shard_map/all_to_all | solution.py:17
  37.3 8.9 %all-to-all-start.1 = ((bf16[4,16,2048]{2,1,0:T(8,128)(2,1)}), bf16[4,16,2048]{2,1,0:T(8,128)(2,1)S(1)}, u32[]{:S(2)}, u32[]{:S(2)}) async-start(bf16[4,16,2048]{2,1,0:T(8,128)(2,1)} %broadcast_in_dim.5), calls=%async_computation.1 | async-start | bytes 524288 | tf_op jit(solution)/shard_map/all_to_all | solution.py:23
  59.2 211.3 %copy-start.5 = (bf16[1,256,2048]{2,1,0:T(8,128)(2,1)S(1)}, bf16[1,256,2048]{2,1,0:T(8,128)(2,1)}, u32[]{:S(2)}) copy-start(bf16[1,256,2048]{2,1,0:T(8,128)(2,1)} %param.15) | copy-start | bytes 3145732
  270.5 1.3 copy-start.6
  278.7 10.7 %copy-start.3 = (f32[64,8]{0,1:T(8,128)S(1)}, f32[64,8]{0,1:T(8,128)}, u32[]{:S(2)}) copy-start(f32[64,8]{0,1:T(8,128)} %param.14) | copy-start | bytes 6148
  278.7 197.5 %all-to-all-start.3 = ((bf16[128,8,2048]{2,1,0:T(8,128)(2,1)}), bf16[128,8,2048]{2,1,0:T(8,128)(2,1)}, u32[]{:S(2)}, u32[]{:S(2)}) async-start(bf16[128,8,2048]{2,1,0:T(8,128)(2,1)} %copy.25), calls=%async_computation.3 | async-start | bytes 8388608 | tf_op jit(solution)/shard_map/all_to_all | solution.py:103
where the time goes:
time: 505 us; the launch traced here: 504 us
  blocking collectives  220 us (44%)
  waiting for transfers between devices  216 us (43%)
  local copies, waits for them, and re-layouts  27.1 us (5%)
  starting transfers between devices  21.9 us (4%)
  other arithmetic  12.1 us (2%)
  matrix products  7.13 us (1%)
    all_to_all x1, blocking collectives, on_device(): lax.all_to_all(outgoing, ('ctx', 'tp'), split_axis=0, concat_axis=0, tile...  211 us
    all_to_all x1, waiting for transfers between devices, on_device(): lax.all_to_all(result.reshape(arrived.shape[0], arrived.shape[1], model_w...  187 us
    all_to_all x1, waiting for transfers between devices, sum_at_owner(): lax.all_to_all(pieces, axis, split_axis=0, concat_axis=0, tiled=True)  24.1 us
    scatter x1, local copies, waits for them, and re-layouts, on_device(): outgoing = jnp.zeros((experts * capacity, model_width), jnp.bfloat16).at[...  12.9 us
    all_to_all x1, starting transfers between devices, on_device(): lax.all_to_all(result.reshape(arrived.shape[0], arrived.shape[1], model_w...  10.7 us
  transfers between devices with their start and end apart: 3, of which 3 were waited for; matrix products, arithmetic and copies ran while one was open for 0% of the time, Pallas kernels for 0%

commit v1 on v0

v1 whole, which is shorter than its diff:
```python
import jax
import jax.numpy as jnp
from jax import lax
from jax.sharding import PartitionSpec as P

EPSILON = 1e-06
F32 = jnp.float32
BF16 = jnp.bfloat16


def on_device(
    attention_out,
    output_weight,
    residual,
    norm_gain,
    routed_experts,
    route_weights,
    gate_weight,
    up_weight,
    down_weight,
):
    rows, width = residual.shape
    top = routed_experts.shape[1]
    replicas = lax.axis_size("dp")
    quarter = rows // replicas
    replica = lax.axis_index("dp")
    experts = lax.axis_size("ctx") * lax.axis_size("tp")
    capacity = min(rows, 2 * rows * top // experts)
    share = capacity // replicas
    down_full = lax.all_gather(down_weight[0], "dp", axis=0, tiled=True)

    partial = jnp.dot(attention_out, output_weight, preferred_element_type=F32).astype(BF16)
    arrived = lax.all_to_all(
        partial.reshape(-1, quarter, width), ("tp", "dp"), split_axis=0, concat_axis=0, tiled=True
    )
    summed = jnp.sum(arrived.astype(F32), axis=0)
    own_residual = lax.dynamic_slice_in_dim(residual, replica * quarter, quarter, 0)
    own_state = own_residual.astype(F32) + summed
    square = jnp.mean(own_state * own_state, axis=-1, keepdims=True)
    own_normed = (own_state * lax.rsqrt(square + EPSILON) * norm_gain).astype(BF16)
    normed = lax.all_gather(own_normed, "dp", axis=0, tiled=True)

    flat_ids = routed_experts.reshape(-1)
    copies = flat_ids.shape[0]
    after = lax.broadcasted_iota(jnp.int32, (copies, copies), 0) > lax.broadcasted_iota(
        jnp.int32, (copies, copies), 1
    )
    before = jnp.sum(((flat_ids[:, None] == flat_ids[None, :]) & after).astype(jnp.int32), axis=1)
    local = before - replica * share
    wanted = jnp.where((local >= 0) & (local < share), flat_ids * share + local, -1)
    wanted = wanted.reshape(rows, top)
    slots = jnp.arange(experts * share, dtype=jnp.int32)
    match = wanted[:, :, None] == slots[None, None, :]
    pick = jnp.any(match, axis=1).astype(BF16)
    outgoing = lax.dot_general(pick, normed, (((0,), (0,)), ((), ())), preferred_element_type=F32)
    outgoing = outgoing.astype(BF16).reshape(experts, share, width)
    incoming = lax.all_to_all(outgoing, ("ctx", "tp"), split_axis=0, concat_axis=0, tiled=True)
    flat_rows = lax.all_gather(incoming.reshape(-1, width), "dp", axis=0, tiled=True)
    gate_act = lax.dot_general(
        flat_rows, gate_weight[0], (((1,), (1,)), ((), ())), preferred_element_type=F32
    )
    up_act = lax.dot_general(
        flat_rows, up_weight[0], (((1,), (1,)), ((), ())), preferred_element_type=F32
    )
    hidden = (jax.nn.silu(gate_act) * up_act).astype(BF16)
    hidden = lax.all_to_all(
        hidden.reshape(replicas, experts * share, -1), "dp", split_axis=0, concat_axis=0, tiled=True
    )
    hidden = jnp.moveaxis(hidden, 0, 1).reshape(experts * share, -1)
    result = jnp.dot(hidden, down_full, preferred_element_type=F32).astype(BF16)
    returned = lax.all_to_all(
        result.reshape(experts, share, width), ("ctx", "tp"), split_axis=0, concat_axis=0, tiled=True
    ).reshape(experts * share, width)
    probs = route_weights / jnp.sum(route_weights, axis=1, keepdims=True)
    spread = jnp.sum(jnp.where(match, probs[:, :, None], 0.0), axis=1)
    high = spread.astype(BF16)
    low = (spread - high.astype(F32)).astype(BF16)
    mixed = jnp.dot(high, returned, preferred_element_type=F32) + jnp.dot(
        low, returned, preferred_element_type=F32
    )
    pieces = mixed.astype(BF16).reshape(replicas, quarter, width)
    pieces = lax.all_to_all(pieces, "dp", 0, 0, tiled=True)
    return (own_state + jnp.sum(pieces.astype(F32), axis=0)).astype(BF16)


def solution(mesh):
    in_specs = (
        P("ctx", ("tp", "dp")),
        P(("tp", "dp"), None),
        P(("ctx", "tp"), None),
        P(),
        P(("ctx", "tp"), None),
        P(("ctx", "tp"), None),
        P(("ctx", "tp"), "dp", None),
        P(("ctx", "tp"), "dp", None),
        P(("ctx", "tp"), "dp", None),
    )
    out_specs = P(("ctx", "tp", "dp"), None)
    return jax.shard_map(
        on_device, mesh=mesh, in_specs=in_specs, out_specs=out_specs, check_vma=False
    )
```

time: 505 us -> 325 us (0.64)
  blocking collectives: 220 us -> 98 us
  waiting for transfers between devices: 216 us -> 162 us
  local copies, waits for them, and re-layouts: 27.1 us -> 6.6 us
  between operations: 0.15 us -> 13.6 us
  other arithmetic: 12.1 us -> 2.7 us
  matrix products: 7.13 us -> 13 us
  starting transfers between devices: 21.9 us -> 27.7 us
    all_to_all x3, waiting for transfers between devices: 216 us -> 68.2 us  [the longest x1 54.9 us: on_device(): lax.all_to_all(result.reshape(experts, share, width), ('ctx', 'tp'), spli...]
    all_to_all x1, blocking collectives: 211 us -> 78.9 us  [on_device(): lax.all_to_all(outgoing, ('ctx', 'tp'), split_axis=0, concat_axis=0, tile...]
    all_gather x0 -> x2, waiting for transfers between devices: none -> 93.4 us  [the longest x1 47.8 us: on_device(): down_full = lax.all_gather(down_weight[0], 'dp', axis=0, tiled=True)]
    scatter x1 -> x0, local copies, waits for them, and re-layouts: 12.9 us -> none  [on_device(): outgoing = jnp.zeros((experts * capacity, model_width), jnp.bfloat16).at[...]
    all_gather x0 -> x1, blocking collectives: none -> 9.37 us  [on_device(): normed = lax.all_gather(own_normed, 'dp', axis=0, tiled=True)]
    gather x1 -> x0, local copies, waits for them, and re-layouts: 8.76 us -> none  [on_device(): returned_flat[slot_index].reshape(row_count, top_count, model_width)]
    reshape x1 -> x0, other arithmetic: 6.48 us -> none  [on_device(): returned_flat = gathered_back.reshape(experts * capacity, model_width)]
    dot_general x4 -> x7, matrix products: 7.13 us -> 13 us  [the longest x1 3.63 us: on_device(): lax.dot_general(flat_rows, gate_weight[0], (((1,), (1,)), ((), ())), pref...]
  transfers between devices with their start and end apart: 3 -> 5, of which waited for: 3 -> 4; matrix products, arithmetic and copies ran while one was open for 0% -> 3% of each run, Pallas kernels for 0% -> 0%
where the time goes in v1:
time: 325 us; the launch traced here: 324 us
  waiting for transfers between devices  162 us (50%)
  blocking collectives  98 us (30%)
  starting transfers between devices  27.7 us (9%)
  between operations  13.6 us (4%)
  matrix products  13 us (4%)
  local copies, waits for them, and re-layouts  6.6 us (2%)
    all_to_all x1, blocking collectives, on_device(): lax.all_to_all(outgoing, ('ctx', 'tp'), split_axis=0, concat_axis=0, tile...  78.9 us
    all_to_all x1, waiting for transfers between devices, on_device(): lax.all_to_all(result.reshape(experts, share, width), ('ctx', 'tp'), spli...  54.9 us
    all_gather x1, waiting for transfers between devices, on_device(): down_full = lax.all_gather(down_weight[0], 'dp', axis=0, tiled=True)  47.8 us
    all_gather x1, waiting for transfers between devices, on_device(): lax.all_gather(incoming.reshape(-1, width), 'dp', axis=0, tiled=True)  45.6 us
    all_to_all x1, starting transfers between devices, on_device(): lax.all_to_all(result.reshape(experts, share, width), ('ctx', 'tp'), spli...  16.6 us
    all_to_all x1, waiting for transfers between devices, on_device(): lax.all_to_all(partial.reshape(-1, quarter, width), ('tp', 'dp'), split_a...  13.3 us
    all_to_all x1, blocking collectives, on_device(): pieces = lax.all_to_all(pieces, 'dp', 0, 0, tiled=True)  9.77 us
    all_gather x1, blocking collectives, on_device(): normed = lax.all_gather(own_normed, 'dp', axis=0, tiled=True)  9.37 us
  transfers between devices with their start and end apart: 5, of which 4 were waited for; matrix products, arithmetic and copies ran while one was open for 3% of the time, Pallas kernels for 0%

profile of v1, /device:TPU:1, one launch (start us, length us, event | category | flops | bytes accessed | tf_op | source)
XLA Modules:
  0.0 324.0 jit_solution(239269866060184144)
XLA Ops:
  6.5 0.0 copy-start
  6.5 0.0 copy-start.2
  6.5 0.0 copy-start.1
  6.5 0.0 copy-start.4
  6.5 1.2 copy-done
  7.8 2.3 convolution_convert_fusion
  10.1 7.6 %all-to-all-start = ((bf16[16,16,2048]{2,1,0:T(8,128)(2,1)}), bf16[16,16,2048]{2,1,0:T(8,128)(2,1)S(1)}, u32[]{:S(2)}, u32[]{:S(2)}) async-start(bf16[16,16,2048]{2,1,0:T(8,128)(2,1)} %bitcast), calls=%async_computation | async-start | bytes 2097152 | tf_op jit(solution)/shard_map/all_to_all | solution.py:33
  17.7 0.0 all-gather.4.cloned.1.call-start
  17.7 0.0 copy-done.2
  17.8 0.1 copy.17
  17.8 0.1 eq.28
  17.9 0.3 convert_reduce_fusion.1
  18.2 0.1 sub.16
  18.3 0.1 copy.19
  18.4 0.2 fusion.11
  18.6 13.3 %all-to-all-done = bf16[16,16,2048]{2,1,0:T(8,128)(2,1)S(1)} async-done(((bf16[16,16,2048]{2,1,0:T(8,128)(2,1)}), bf16[16,16,2048]{2,1,0:T(8,128)(2,1)S(1)}, u32[]{:S(2)}, u32[]{:S(2)}) %all-to-all-start) | async-done | bytes 1048608 | tf_op jit(solution)/shard_map/all_to_all | solution.py:33
  31.9 0.1 convert_reduce_fusion
  32.1 0.0 copy-done.1
  32.1 0.1 multiply_reduce_fusion
  32.2 0.0 copy-done.4
  32.2 0.1 multiply_convert_fusion
  32.3 9.4 %all_gather.9 = bf16[64,2048]{1,0:T(8,128)(2,1)S(1)} all-gather(bf16[16,2048]{1,0:T(8,128)(2,1)S(1)} %multiply_convert_fusion), channel_id=1, replica_groups=mesh['ctx'=32,'tp'=4,'dp'=4] {'dp'}, dimensions={0}, use_global_device_ids=true | all-gather | bytes 327680 | tf_op jit(solution)/shard_map/all_gather | solution.py:41
  41.7 0.5 convolution_convert_fusion.1
  42.2 0.7 reshape.52
  42.9 78.9 %all_to_all.25 = bf16[128,2,2048]{2,1,0:T(2,128)(2,1)S(1)} all-to-all(bf16[128,2,2048]{2,1,0:T(2,128)(2,1)S(1)} %reshape.52), channel_id=1, replica_groups=mesh['ctx'=32,'tp'=4,'dp'=4] {'ctx','tp'}, dimensions={0} | all-to-all | bytes 2097152 | tf_op jit(solution)/shard_map/all_to_all | solution.py:57
  121.8 0.0 copy-start.6
  121.8 1.3 reshape.53
  123.1 0.0 all-gather.4.cloned.1.call-update
  123.1 0.0 all-gather.6.cloned.1.call-start
  123.2 0.7 all-gather.6.cloned.1.call-update
  123.9 45.6 %all-gather.4.cloned.1.call-done = bf16[1024,2048]{1,0:T(8,128)(2,1)} async-done(((bf16[256,2048]{1,0:T(8,128)(2,1)}), bf16[1024,2048]{1,0:T(8,128)(2,1)}) %all-gather.4.cloned.1.call-update) | async-done | bytes 4194320 | tf_op jit(solution)/shard_map/all_gather | solution.py:58
  169.5 0.0 copy-done.6
  169.5 0.0 copy-start.5
  169.5 3.6 %fusion.8 = f32[1024,256]{1,0:T(8,128)S(1)} fusion(bf16[1024,2048]{1,0:T(8,128)(2,1)} %all-gather.4.cloned.1.call-done, bf16[1,256,2048]{2,1,0:T(8,128)(2,1)S(1)} %copy-done.6), kind=kOutput, calls=%fused_computation.11 | convolution fusion | flops 1073741824 | bytes 6291456 | tf_op jit(solution)/shard_map/dot_general | solution.py:59
  173.1 0.0 copy-done.5
  173.1 2.5 fusion.6
  175.7 1.0 copy.21
  176.7 3.5 %all-to-all-start.2 = ((bf16[4,256,256]{1,2,0:T(8,128)(2,1)}), bf16[4,256,256]{1,2,0:T(8,128)(2,1)S(1)}, u32[]{:S(2)}, u32[]{:S(2)}) async-start(bf16[4,256,256]{1,2,0:T(8,128)(2,1)} %copy.21), calls=%async_computation.2 | async-start | bytes 1048576 | tf_op jit(solution)/shard_map/all_to_all | solution.py:66
  180.1 47.8 %all-gather.6.cloned.1.call-done = bf16[1,1024,2048]{2,1,0:T(8,128)(2,1)} async-done(((bf16[1,256,2048]{2,1,0:T(8,128)(2,1)}), bf16[1,1024,2048]{2,1,0:T(8,128)(2,1)}) %all-gather.6.cloned.1.call-update) | async-done | bytes 4194320 | tf_op jit(solution)/shard_map/all_gather | solution.py:30
  228.0 0.0 all-to-all-done.2
  228.0 0.0 copy-start.3
  228.0 3.5 %fusion.2 = bf16[256,2048]{1,0:T(8,128)(2,1)S(1)} fusion(bf16[256,1024]{0,1:T(8,128)(2,1)S(1)} %bitcast.27, bf16[1,1024,2048]{2,1,0:T(8,128)(2,1)} %all-gather.6.cloned.1.call-done), kind=kOutput, calls=%fused_computation.2 | convolution fusion | flops 1074266112 | bytes 5767168 | tf_op jit(solution)/shard_map/dot_general | solution.py:70
  231.4 1.5 reshape.56
  233.0 16.6 %all-to-all-start.3 = ((bf16[128,2,2048]{2,1,0:T(2,128)(2,1)}), bf16[128,2,2048]{2,1,0:T(2,128)(2,1)S(1)}, u32[]{:S(2)}, u32[]{:S(2)}) async-start(bf16[128,2,2048]{2,1,0:T(2,128)(2,1)} %reshape.56), calls=%async_computation.3 | async-start | bytes 2097152 | tf_op jit(solution)/shard_map/all_to_all | solution.py:71
  249.6 0.0 copy-done.3
  249.6 0.1 copy.20
  249.7 0.2 select_reduce_fusion
  249.9 54.9 %all-to-all-done.3 = bf16[128,2,2048]{2,1,0:T(2,128)(2,1)S(1)} async-done(((bf16[128,2,2048]{2,1,0:T(2,128)(2,1)}), bf16[128,2,2048]{2,1,0:T(2,128)(2,1)S(1)}, u32[]{:S(2)}, u32[]{:S(2)}) %all-to-all-start.3) | async-done | bytes 1048608 | tf_op jit(solution)/shard_map/all_to_all | solution.py:71
  304.8 0.4 reshape.57
  305.3 0.3 fusion.13
  305.6 0.3 fusion.5
  305.9 9.8 %all_to_all.26 = bf16[4,16,2048]{2,1,0:T(8,128)(2,1)S(1)} all-to-all(bf16[4,16,2048]{2,1,0:T(8,128)(2,1)S(1)} %bitcast.26), channel_id=1, replica_groups=mesh['ctx'=32,'tp'=4,'dp'=4] {'dp'}, dimensions={0} | all-to-all | bytes 524288 | tf_op jit(solution)/shard_map/all_to_all | solution.py:82
  315.7 1.5 add_convert_fusion
  (7 shorter events, 0.1 us)
Async XLA Ops:
  6.5 1.2 copy-start
  6.5 11.2 %copy-start.2 = (s32[64,8]{0,1:T(8,128)S(1)}, s32[64,8]{0,1:T(8,128)}, u32[]{:S(2)}) copy-start(s32[64,8]{0,1:T(8,128)} %param.13) | copy-start | bytes 6148
  6.5 25.5 %copy-start.1 = (bf16[64,2048]{1,0:T(8,128)(2,1)S(1)}, bf16[64,2048]{1,0:T(8,128)(2,1)}, u32[]{:S(2)}) copy-start(bf16[64,2048]{1,0:T(8,128)(2,1)} %param.11) | copy-start | bytes 786436
  6.5 25.7 %copy-start.4 = (f32[2048]{0:T(1024)S(1)}, f32[2048]{0:T(1024)}, u32[]{:S(2)}) copy-start(f32[2048]{0:T(1024)} %param.12) | copy-start | bytes 24580
  10.1 21.8 %all-to-all-start = ((bf16[16,16,2048]{2,1,0:T(8,128)(2,1)}), bf16[16,16,2048]{2,1,0:T(8,128)(2,1)S(1)}, u32[]{:S(2)}, u32[]{:S(2)}) async-start(bf16[16,16,2048]{2,1,0:T(8,128)(2,1)} %bitcast), calls=%async_computation | async-start | bytes 2097152 | tf_op jit(solution)/shard_map/all_to_all | solution.py:33
  17.7 151.8 %all-gather.4.cloned.1.call-start = ((), (), s32[]{:S(2)}) async-start(), calls=%async_computation.5 | async-start | bytes 5242880 | tf_op jit(solution)/shard_map/all_gather | solution.py:58
  121.8 47.7 %copy-start.6 = (bf16[1,256,2048]{2,1,0:T(8,128)(2,1)S(1)}, bf16[1,256,2048]{2,1,0:T(8,128)(2,1)}, u32[]{:S(2)}) copy-start(bf16[1,256,2048]{2,1,0:T(8,128)(2,1)} %param.15) | copy-start | bytes 3145732
  123.1 104.9 %all-gather.6.cloned.1.call-start = ((), (), s32[]{:S(2)}) async-start(), calls=%async_computation.6 | async-start | bytes 5242880 | tf_op jit(solution)/shard_map/all_gather | solution.py:30
  169.5 3.6 %copy-start.5 = (bf16[1024,2048]{1,0:T(8,128)(2,1)S(1)}, bf16[1024,2048]{1,0:T(8,128)(2,1)}, u32[]{:S(2)}) copy-start(bf16[1024,2048]{1,0:T(8,128)(2,1)} %all-gather.4.cloned.1.call-done) | copy-start | bytes 12582916
  176.7 51.3 %all-to-all-start.2 = ((bf16[4,256,256]{1,2,0:T(8,128)(2,1)}), bf16[4,256,256]{1,2,0:T(8,128)(2,1)S(1)}, u32[]{:S(2)}, u32[]{:S(2)}) async-start(bf16[4,256,256]{1,2,0:T(8,128)(2,1)} %copy.21), calls=%async_computation.2 | async-start | bytes 1048576 | tf_op jit(solution)/shard_map/all_to_all | solution.py:66
  228.0 21.6 %copy-start.3 = (f32[64,8]{0,1:T(8,128)S(1)}, f32[64,8]{0,1:T(8,128)}, u32[]{:S(2)}) copy-start(f32[64,8]{0,1:T(8,128)} %param.14) | copy-start | bytes 6148
  233.0 71.9 %all-to-all-start.3 = ((bf16[128,2,2048]{2,1,0:T(2,128)(2,1)}), bf16[128,2,2048]{2,1,0:T(2,128)(2,1)S(1)}, u32[]{:S(2)}, u32[]{:S(2)}) async-start(bf16[128,2,2048]{2,1,0:T(2,128)(2,1)} %reshape.56), calls=%async_computation.3 | async-start | bytes 2097152 | tf_op jit(solution)/shard_map/all_to_all | solution.py:71
Sparse Core Ops, SparseCore 0:
  123.2 46.1 all-gather.3
  171.6 56.3 all-gather.5

commit v2 on v1

v2 whole, which is shorter than its diff:
```python
import functools
import jax
import jax.numpy as jnp
from jax import lax
from jax.experimental import pallas as pl
from jax.experimental.pallas import tpu as pltpu
from jax.sharding import PartitionSpec as P

EPSILON = 1e-06
F32 = jnp.float32
BF16 = jnp.bfloat16
MESH = pl.DeviceIdType.MESH
CAP = 8
CORES = 2
CHUNKS = 4
NT = (((1,), (1,)), ((), ()))


def kernel(
    size,
    attn_ref,
    weight_ref,
    residual_ref,
    gain_ref,
    ids_ref,
    choice_ref,
    gate_ref,
    up_ref,
    down_ref,
    out_ref,
    gate_v,
    up_v,
    down_v,
    part0,
    part1,
    first0,
    first1,
    sum0,
    sum1,
    last0,
    last1,
    state,
    normed,
    tokens,
    meta,
    mix,
    packed,
    gathered,
    hidden_out,
    hidden,
    answers,
    returned,
    partial,
    chain_in,
    chain_out,
    final,
    finished,
    local_sem,
    a0s, a0r, a1s, a1r, b0s, b0r, b1s, b1r,
    ns, nr,
    ds, dr,
    zs, zr, ms, mr,
    xs, xr,
    ys, yr,
    hs, hr,
    rs, rr,
    qs, qr,
    fs, fr,
):
    nz, nc, nx, ny = size
    units = nc * nx
    turns = nz // ny
    half_ring = nz // 2
    ctx, x, y = lax.axis_index("ctx"), lax.axis_index("tp"), lax.axis_index("dp")
    z, c = lax.div(ctx, nc), lax.rem(ctx, nc)
    me = c * nx + x
    own, width = out_ref.shape
    rows = own * ny
    half = width // 2
    share = gate_v.shape[0]
    block = 2 * rows
    piece = block // CHUNKS
    unit = 2 * CAP
    sends = []

    def remote(src, dst, send_sem, recv_sem, device):
        return pltpu.make_async_remote_copy(
            src_ref=src, dst_ref=dst, send_sem=send_sem, recv_sem=recv_sem,
            device_id=device, device_id_type=MESH,
        )

    def send(src, dst, send_sem, recv_sem, device, when=None):
        copy = remote(src, dst, send_sem, recv_sem, device)
        if when is None:
            copy.start()
        else:
            @pl.when(when)
            def _():
                copy.start()
        sends.append((when, copy))

    def arrived(dst, recv_sem):
        remote(dst, dst, local_sem.at[3], recv_sem, ahead).wait_recv()

    def y_of(step):
        return lax.rem(y + step, ny)

    ahead = (lax.rem(z + 1, nz) * nc + c, x, y)
    behind = (lax.rem(z + nz - 1, nz) * nc + c, x, y)
    x_steps = [(0, dx) for dx in range(1, nx)]
    plane_steps = [(dc, dx) for dc in range(nc) for dx in range(nx) if (dc, dx) != (0, 0)]

    def plane_peer(step):
        pc, px = lax.rem(c + step[0], nc), lax.rem(x + step[1], nx)
        return pc * nx + px, (z * nc + pc, px, y)

    peers = [ahead, behind]
    peers += [plane_peer(s)[1] for s in plane_steps]
    peers += [(ctx, x, y_of(s)) for s in range(1, ny)]
    barrier = pltpu.get_barrier_semaphore()
    for peer in peers:
        pl.semaphore_signal(barrier, inc=1, device_id=peer, device_id_type=MESH)

    def down_rows(at_y, part=0, parts=1):
        count = share // parts
        return down_v.at[pl.ds(pl.multiple_of(at_y * share + part * count, count), count)]

    local = [
        pltpu.make_async_copy(gate_ref, gate_v, local_sem.at[0]),
        pltpu.make_async_copy(up_ref, up_v, local_sem.at[1]),
        pltpu.make_async_copy(down_ref, down_rows(y), local_sem.at[2]),
    ]
    for copy in (local[2], local[0], local[1]):
        copy.start()

    attn = attn_ref[...]
    cols = half // 2
    for j in range(2):
        at = pl.ds(j * cols, cols)
        prod = jnp.dot(attn, weight_ref[:, at], preferred_element_type=F32).astype(BF16)
        for px in range(nx):
            for py in range(ny):
                lo = px * rows + py * own
                part0[py, px, :, at] = prod[lo : lo + own]
    pl.semaphore_wait(barrier, len(peers))
    for s in range(1, ny):
        py = y_of(s)
        send(part0.at[py], first0.at[y], a0s.at[py], a0r.at[y], (ctx, x, py))
    for j in range(2):
        at = pl.ds(j * cols, cols)
        prod = jnp.dot(
            attn, weight_ref[:, pl.ds(half + j * cols, cols)], preferred_element_type=F32
        ).astype(BF16)
        for px in range(nx):
            for py in range(ny):
                lo = px * rows + py * own
                part1[px, py, :, at] = prod[lo : lo + own]
    for s in x_steps:
        px = lax.rem(x + s[1], nx)
        send(part1.at[px], first1.at[x], a1s.at[px], a1r.at[x], (ctx, px, y))

    ids = ids_ref[...].astype(F32)
    top = ids.shape[0]
    experts = nz * units
    expert_row = lax.broadcasted_iota(jnp.int32, (experts, block), 0).astype(F32)
    named = jnp.zeros((experts, block), F32)
    for k in range(top):
        named = jnp.where(ids[k : k + 1] == expert_row, 1.0, named)
    from_row = lax.broadcasted_iota(jnp.int32, (block, block), 0)
    to_row = lax.broadcasted_iota(jnp.int32, (block, block), 1)
    earlier = jnp.where(
        jnp.logical_or(
            from_row < jnp.minimum(to_row, rows),
            jnp.logical_and(from_row < to_row - rows, from_row < rows),
        ),
        1.0,
        0.0,
    )
    earlier = jnp.where(
        jnp.logical_and(to_row >= rows, from_row >= to_row - rows), 0.0, earlier
    )
    count = jnp.dot(named.astype(BF16), earlier.astype(BF16), preferred_element_type=F32)
    slots = jnp.concatenate(
        [
            jnp.sum(jnp.where(ids[k : k + 1] == expert_row, count, 0.0), axis=0, keepdims=True)
            for k in range(top)
        ],
        axis=0,
    )
    choice = choice_ref[...]
    probs = choice / jnp.sum(choice, axis=0, keepdims=True)
    high = probs.astype(BF16).astype(F32)
    turn_own = lax.div(z, ny)
    y_own = lax.rem(z, ny)
    routing = jnp.concatenate([ids, slots, high, probs - high], axis=0).astype(BF16)
    is_owner = y == y_own

    @pl.when(is_owner)
    def _():
        meta[turn_own] = routing

    local[2].wait()
    for i, s in enumerate((1, ny - 1) if ny > 2 else (1,)):
        py = y_of(s)
        send(down_rows(y), down_rows(y), ds.at[i], dr.at[y, 0], (ctx, x, py))

    for s in range(1, ny):
        py = y_of(s)
        arrived(first0.at[py], a0r.at[py])
    for px in range(nx):
        total = part0[y, px].astype(F32)
        for s in range(1, ny):
            total += first0[y_of(s), px].astype(F32)
        sum0[px] = total.astype(BF16)
    for s in x_steps:
        px = lax.rem(x + s[1], nx)
        send(sum0.at[px], last0.at[x], b0s.at[px], b0r.at[x], (ctx, px, y))
    for s in x_steps:
        px = lax.rem(x + s[1], nx)
        arrived(first1.at[px], a1r.at[px])
    for py in range(ny):
        total = part1[x, py].astype(F32)
        for s in x_steps:
            total += first1[lax.rem(x + s[1], nx), py].astype(F32)
        sum1[py] = total.astype(BF16)
    for s in range(1, ny):
        py = y_of(s)
        send(sum1.at[py], last1.at[y], b1s.at[py], b1r.at[y], (ctx, x, py))
    mine = pl.ds(pl.multiple_of(y * own, own), own)
    low_sum = sum0[x].astype(F32) + residual_ref[mine, :half].astype(F32)
    high_sum = sum1[y].astype(F32) + residual_ref[mine, half:].astype(F32)
    for s in x_steps:
        px = lax.rem(x + s[1], nx)
        arrived(last0.at[px], b0r.at[px])
        low_sum += last0[px].astype(F32)
    for s in range(1, ny):
        py = y_of(s)
        arrived(last1.at[py], b1r.at[py])
        high_sum += last1[py].astype(F32)
    state[0] = low_sum
    state[1] = high_sum
    square = (
        jnp.sum(low_sum * low_sum, axis=-1, keepdims=True)
        + jnp.sum(high_sum * high_sum, axis=-1, keepdims=True)
    ) / width
    scale = lax.rsqrt(square + EPSILON)
    normed[0] = (low_sum * scale * gain_ref[:, :half]).astype(BF16)
    normed[1] = (high_sum * scale * gain_ref[:, half:]).astype(BF16)

    for h in range(2):
        place = pl.ds(pl.multiple_of(h * rows + y * own, own), own)
        send(
            normed.at[h], tokens.at[turn_own, place, :], ns.at[h], nr.at[y, h],
            (ctx, x, y_own), when=y != y_own,
        )

    @pl.when(is_owner)
    def _():
        for h in range(2):
            place = pl.ds(pl.multiple_of(h * rows + y * own, own), own)
            tokens[turn_own, place, :] = normed[h]
        for s in range(1, ny):
            py = y_of(s)
            for h in range(2):
                place = pl.ds(pl.multiple_of(h * rows + py * own, own), own)
                arrived(tokens.at[turn_own, place, :], nr.at[py, h])

    def turn(r, at_y):
        off = lax.rem(z + ny - at_y, ny)
        late = lax.div(2 * off, ny + 1)
        if turns == 4:
            near, far = ((0, 3), (3, 0), (1, 2), (2, 1))[r]
        elif turns == 2:
            near, far = ((0, 1), (1, 0))[r]
        else:
            near, far = 0, 0
        distance = off + ny * (near + (far - near) * late)
        return lax.div(lax.rem(z + nz - distance, nz), ny), distance

    my_turns = [turn(r, y) for r in range(turns)]

    def z_step(r, k):
        t, d = my_turns[r]
        at = pl.ds(k * piece, piece)
        ref, sem = tokens.at[t, at, :], zr.at[t, k]

        @pl.when(d > 0)
        def _():
            arrived(ref, sem)
            if k == 0:
                arrived(meta.at[t], mr.at[t])

        forward, backward = d < half_ring, jnp.logical_or(d == 0, d > half_ring + 1)
        for way, (go, device) in enumerate(((forward, ahead), (backward, behind))):
            send(ref, ref, zs.at[way, t, k], sem, device, when=go)
            if k == 0:
                send(meta.at[t], meta.at[t], ms.at[way, t], mr.at[t], device, when=go)

    slot_row = lax.broadcasted_iota(jnp.int32, (unit, block), 0)
    token_lane = lax.broadcasted_iota(jnp.int32, (unit, block), 1)
    same_half = lax.div(slot_row, CAP) == lax.div(token_lane, rows)
    slot_want = jnp.where(same_half, lax.rem(slot_row, CAP), -2).astype(F32)

    def pack(r):
        t, _ = my_turns[r]
        table = meta[t].astype(F32)
        first = (z * units).astype(F32)
        picks, highs, lows = [], [], []
        for u in range(units):
            got = jnp.full((unit, block), -1.0, F32)
            big = jnp.zeros((unit, block), F32)
            small = jnp.zeros((unit, block), F32)
            for k in range(top):
                hit = table[k : k + 1] == first + float(u)
                got = jnp.where(hit, table[top + k : top + k + 1], got)
                big = jnp.where(hit, table[2 * top + k : 2 * top + k + 1], big)
                small = jnp.where(hit, table[3 * top + k : 3 * top + k + 1], small)
            hit = got == slot_want
            picks.append(jnp.where(hit, 1.0, 0.0))
            highs.append(jnp.where(hit, big, 0.0))
            lows.append(jnp.where(hit, small, 0.0))
        chosen = jnp.concatenate(picks, axis=0).astype(BF16)
        mix[t, 0] = jnp.concatenate(highs, axis=0).T.astype(BF16)
        mix[t, 1] = jnp.concatenate(lows, axis=0).T.astype(BF16)
        for j in range(2):
            at = pl.ds(j * cols, cols)
            out = jnp.dot(chosen, tokens[t, :, at], preferred_element_type=F32)
            packed[t, :, :, at] = out.astype(BF16).reshape(units, unit, cols)
        for i, s in enumerate(plane_steps):
            index, device = plane_peer(s)
            send(
                packed.at[t, index], gathered.at[y, t, me], xs.at[t, i], xr.at[t, me], device
            )
        gathered[y, t, me] = packed[t, me]

    def y_send(r):
        t, _ = my_turns[r]
        for s in plane_steps:
            index, _ = plane_peer(s)
            arrived(gathered.at[y, t, index], xr.at[t, index])
        for i, s in enumerate((1, ny - 1) if ny > 2 else (1,)):
            send(
                gathered.at[y, t], gathered.at[y, t], ys.at[i, t], yr.at[y, t, 0],
                (ctx, x, y_of(s)),
            )

    def y_forward(r):
        for i, s in enumerate((ny - 1, 1) if ny > 2 else (1,)):
            py = y_of(s)
            t, _ = turn(r, py)
            arrived(gathered.at[py, t], yr.at[py, t, 0])
            if ny > 2:
                part = gathered.at[py, t, pl.ds(i * (units // 2), units // 2)]
                send(part, part, ys.at[2 + i, t], yr.at[py, t, 1 + i], (ctx, x, y_of(ny - s)))

    def y_last(r):
        if ny > 2:
            py = y_of(2)
            t, _ = turn(r, py)
            for i in range(2):
                part = gathered.at[py, t, pl.ds(i * (units // 2), units // 2)]
                arrived(part, yr.at[py, t, 1 + i])

    def d_forward():
        for i, s in enumerate((ny - 1, 1) if ny > 2 else (1,)):
            py = y_of(s)
            arrived(down_rows(py), dr.at[py, 0])
            if ny > 2:
                part = down_rows(py, i, 2)
                send(part, part, ds.at[2 + i], dr.at[py, 1 + i], (ctx, x, y_of(ny - s)))

    def d_last():
        if ny > 2:
            py = y_of(2)
            for i in range(2):
                part = down_rows(py, i, 2)
                arrived(part, dr.at[py, 1 + i])

    def expert(r, s):
        py = y_of(s)
        t, _ = turn(r, py)
        data = gathered[py, t].reshape(units * unit, half)

        def both(weights):
            low = lax.dot_general(data, weights[:, :half], NT, preferred_element_type=F32)
            high = lax.dot_general(data, weights[:, half:], NT, preferred_element_type=F32)
            low = low.reshape(units, unit, share)[:, :CAP]
            return low + high.reshape(units, unit, share)[:, CAP:]

        gate_act = both(gate_v)
        up_act = both(up_v)
        act = gate_act / (1.0 + jnp.exp(-gate_act)) * up_act
        act = act.reshape(units * CAP, share).astype(BF16)
        place = pl.ds(pl.multiple_of(y * share, share), share)
        if s == 0:
            hidden[t, :, place] = act
        else:
            hidden_out[s - 1, r] = act
            send(
                hidden_out.at[s - 1, r], hidden.at[t, :, place], hs.at[s - 1, r], hr.at[y, t],
                (ctx, x, py),
            )

    if turns == 4:
        for k in range(CHUNKS):
            z_step(0, k)
            z_step(1, k)
        pack(0)
        pack(1)
        for k in range(CHUNKS):
            z_step(2, k)
            z_step(3, k)
            if k == 1:
                y_send(0)
        y_send(1)
        pack(2)
        pack(3)
        d_forward()
        y_forward(0)
        y_send(2)
        local[0].wait()
        local[1].wait()
        expert(0, 0)
        y_forward(1)
        y_send(3)
        expert(1, 0)
        expert(0, 1)
        expert(0, 3)
        y_last(0)
        expert(0, 2)
        y_forward(2)
        expert(1, 1)
        expert(1, 3)
        expert(2, 0)
        y_last(1)
        expert(1, 2)
        y_forward(3)
        expert(3, 0)
        expert(2, 1)
        expert(2, 3)
        y_last(2)
        expert(2, 2)
        expert(3, 1)
        expert(3, 3)
        y_last(3)
        expert(3, 2)
    else:
        for k in range(CHUNKS):
            for r in range(turns):
                z_step(r, k)
        for r in range(turns):
            pack(r)
        d_forward()
        local[0].wait()
        local[1].wait()
        for r in range(turns):
            y_send(r)
        for r in range(turns):
            y_forward(r)
        for r in range(turns):
            y_last(r)
            for s in range(ny):
                expert(r, s)
    d_last()

    def answer(r):
        t, _ = my_turns[r]
        for s in range(1, ny):
            py = y_of(s)
            arrived(hidden.at[t, :, pl.ds(pl.multiple_of(py * share, share), share)], hr.at[py, t])
        data = hidden[t]
        step = half // 4
        for j in range(4):
            low = jnp.dot(data, down_v[:, pl.ds(j * step, step)], preferred_element_type=F32)
            high = jnp.dot(data, down_v[:, pl.ds(half + j * step, step)], preferred_element_type=F32)
            low = low.reshape(units, CAP, step)
            high = high.reshape(units, CAP, step)
            both = jnp.concatenate([low, high], axis=1)
            answers[t, :, :, pl.ds(j * step, step)] = both.astype(BF16)
        for i, s in enumerate(plane_steps):
            index, device = plane_peer(s)
            send(answers.at[t, index], returned.at[t, me], rs.at[t, i], rr.at[t, me], device)
        returned[t, me] = answers[t, me]

    def combine(r):
        t, _ = my_turns[r]
        for s in plane_steps:
            index, _ = plane_peer(s)
            arrived(returned.at[t, index], rr.at[t, index])
        for j in range(2):
            at = pl.ds(j * cols, cols)
            data = returned[t, :, :, at].reshape(units * unit, cols)
            partial[t, :, at] = jnp.dot(
                mix[t, 0], data, preferred_element_type=F32
            ) + jnp.dot(mix[t, 1], data, preferred_element_type=F32)

    def z_reduce(r, k):
        t, d = my_turns[r]
        at = pl.ds(k * piece, piece)
        onward = lax.div(d, half_ring + 1)
        next_z = lax.rem(z + nz + 2 * onward - 1, nz)
        slot = t + (turns - t) * lax.div(d, nz - 1)
        starts = jnp.logical_or(d == half_ring, d == half_ring + 1)

        @pl.when(starts)
        def _():
            chain_out[t, at, :] = partial[t, at, :].astype(BF16)

        @pl.when(jnp.logical_not(starts))
        def _():
            arrived(chain_in.at[t, at, :], qr.at[t, k])
            total = partial[t, at, :] + chain_in[t, at, :].astype(F32)
            if r < 2:
                partial[t, at, :] = total
            chain_out[t, at, :] = total.astype(BF16)

        send(
            chain_out.at[t, at, :], chain_in.at[slot, at, :], qs.at[t, k], qr.at[slot, k],
            (next_z * nc + c, x, y), when=d > 0,
        )
        if r < 2:
            @pl.when(d == 0)
            def _():
                arrived(chain_in.at[turns, at, :], qr.at[turns, k])
                total = partial[t, at, :] + chain_in[turns, at, :].astype(F32)
                final[at, :] = total.astype(BF16)

    def hand_out():
        for h in range(2):
            for py in range(ny):
                place = pl.ds(h * rows + py * own, own)
                send(
                    final.at[place, :], finished.at[h], fs.at[h, py], fr.at[h], (ctx, x, py),
                    when=jnp.logical_and(is_owner, y != py),
                )

    if turns == 4:
        for r in (3, 2, 1, 0):
            answer(r)
        combine(3)
        combine(2)
        for k in range(CHUNKS):
            z_reduce(3, k)
            z_reduce(2, k)
            if k == 0:
                combine(1)
                combine(0)
        for k in range(CHUNKS):
            z_reduce(1, k)
            z_reduce(0, k)
    else:
        for r in range(turns - 1, -1, -1):
            answer(r)
        for r in range(turns - 1, -1, -1):
            combine(r)
        for k in range(CHUNKS):
            for r in range(turns - 1, -1, -1):
                z_reduce(r, k)
    hand_out()

    @pl.when(is_owner)
    def _():
        for h in range(2):
            place = pl.ds(pl.multiple_of(h * rows + y * own, own), own)
            finished[h] = final[place, :]

    @pl.when(jnp.logical_not(is_owner))
    def _():
        for h in range(2):
            arrived(finished.at[h], fr.at[h])

    for h in range(2):
        out_ref[:, pl.ds(h * half, half)] = (state[h] + finished[h].astype(F32)).astype(BF16)

    for when, copy in sends:
        if when is None:
            copy.wait_send()
        else:
            @pl.when(when)
            def _():
                copy.wait_send()


def on_device(
    size,
    attention_out,
    output_weight,
    residual,
    norm_gain,
    routed_experts,
    route_weights,
    gate_weight,
    up_weight,
    down_weight,
):
    nz, nc, nx, ny = size
    rows, width = residual.shape
    own, half = rows // ny, width // 2
    share = gate_weight.shape[1]
    top = routed_experts.shape[1]
    units, turns, unit, block = nc * nx, nz // ny, 2 * CAP, 2 * rows
    ids = jnp.concatenate([routed_experts.T, routed_experts.T], axis=1)
    choice = jnp.concatenate([route_weights.T, route_weights.T], axis=1)

    def vmem(*shape, dtype=BF16):
        return pltpu.VMEM(shape, dtype)

    def sems(*shape):
        return pltpu.SemaphoreType.DMA(shape)

    whole = pl.BlockSpec(memory_space=pltpu.VMEM)
    far = pl.BlockSpec(memory_space=pl.ANY)
    return pl.pallas_call(
        functools.partial(kernel, size),
        out_shape=jax.ShapeDtypeStruct((own, width), BF16),
        in_specs=[whole] * 6 + [far] * 3,
        out_specs=whole,
        scratch_shapes=[
            vmem(share, width),
            vmem(share, width),
            vmem(ny * share, width),
            vmem(ny, nx, own, half),
            vmem(nx, ny, own, half),
            vmem(ny, nx, own, half),
            vmem(nx, ny, own, half),
            vmem(nx, own, half),
            vmem(ny, own, half),
            vmem(nx, own, half),
            vmem(ny, own, half),
            vmem(2, own, half, dtype=F32),
            vmem(2, own, half),
            vmem(turns, block, half),
            vmem(turns, 4 * top, block),
            vmem(turns, 2, block, units * unit),
            vmem(turns, units, unit, half),
            vmem(ny, turns, units, unit, half),
            vmem(ny - 1, turns, units * CAP, share),
            vmem(turns, units * CAP, ny * share),
            vmem(turns, units, unit, half),
            vmem(turns, units, unit, half),
            vmem(turns, block, half, dtype=F32),
            vmem(turns + 1, block, half),
            vmem(turns, block, half),
            vmem(block, half),
            vmem(2, own, half),
            sems(4),
            sems(ny), sems(ny), sems(nx), sems(nx), sems(nx), sems(nx), sems(ny), sems(ny),
            sems(2), sems(ny, 2),
            sems(4), sems(ny, 3),
            sems(2, turns, CHUNKS), sems(turns, CHUNKS), sems(2, turns), sems(turns),
            sems(turns, units), sems(turns, units),
            sems(4, turns), sems(ny, turns, 3),
            sems(ny, turns), sems(ny, turns),
            sems(turns, units), sems(turns, units),
            sems(turns, CHUNKS), sems(turns + 1, CHUNKS),
            sems(2, ny), sems(2),
        ],
        compiler_params=pltpu.CompilerParams(
            collective_id=0, has_side_effects=True, vmem_limit_bytes=56 * 1024 * 1024
        ),
    )(
        attention_out, output_weight, residual, norm_gain.reshape(1, -1), ids, choice,
        gate_weight[0], up_weight[0], down_weight[0],
    )


def solution(mesh):
    nc = min(CORES, mesh.shape["ctx"])
    size = (mesh.shape["ctx"] // nc, nc, mesh.shape["tp"], mesh.shape["dp"])
    in_specs = (
        P("ctx", ("tp", "dp")),
        P(("tp", "dp"), None),
        P(("ctx", "tp"), None),
        P(),
        P(("ctx", "tp"), None),
        P(("ctx", "tp"), None),
        P(("ctx", "tp"), "dp", None),
        P(("ctx", "tp"), "dp", None),
        P(("ctx", "tp"), "dp", None),
    )
    out_specs = P(("ctx", "tp", "dp"), None)
    return jax.shard_map(
        functools.partial(on_device, size),
        mesh=mesh, in_specs=in_specs, out_specs=out_specs, check_vma=False,
    )
```

time: 325 us -> 339 us (1.043)
  the two profiles are of different devices: /device:TPU:1 before, /device:TPU:96 now
where the time goes in v2:
time: 339 us
  Pallas kernels  335 us (99%)
    pallas_call x1, Pallas kernels, on_device(): pl.pallas_call(functools.partial(kernel, size), out_shape=jax.ShapeDtypeS...  335 us

profile of v2, /device:TPU:96, one launch (start us, length us, event | category | flops | bytes accessed | tf_op | source)
XLA Modules:
  0.0 338.9 jit_solution(8049959073979081609)
XLA Ops:
  0.0 0.0 copy-start
  0.0 0.7 copy-done
  0.7 0.0 copy-start.1
  0.7 0.7 pad_add_fusion.ids_ref
  1.4 0.0 copy-done.1
  1.4 0.7 pad_maximum_fusion.choice_ref
  2.0 335.4 %shard_map.91 = bf16[16,2048]{1,0:T(8,128)(2,1)} custom-call(bf16[256,256]{1,0:T(8,128)(2,1)} %attn_ref.1, bf16[256,2048]{1,0:T(8,128)(2,1)} %weight_ref.1, bf16[64,2048]{1,0:T(8,128)(2,1)} %residual_ref.1, f32[1,2048]{1,0:T(1,128)} %bitcast.9, s32[8,128]{1,0:T(8,128)} %pad_add_fusion.ids_ref, f32[8,128]{1,0:T(8,128)} %pad_maximum_fusion.choice_ref, ...), custom_call_target="tpu_custom_call" | custom-call | tf_op jit(solution)/shard_map/pallas_call | solution.py:613
  337.4 1.5 copy.11
Async XLA Ops:
  0.0 0.7 copy-start
  0.7 0.7 copy-start.1

commit v3 on v2

--- a/solution.py
+++ b/solution.py
@@ -13,6 +13,7 @@
 CAP = 8
 CORES = 2
 CHUNKS = 4
+HOP = 3
 NT = (((1,), (1,)), ((), ()))
 
 
@@ -159,6 +160,12 @@
         px = lax.rem(x + s[1], nx)
         send(part1.at[px], first1.at[x], a1s.at[px], a1r.at[x], (ctx, px, y))
 
+    def d_send(second):
+        for i, s in enumerate((1, ny - 1) if ny > 2 else (1,)):
+            j = 1 - i if second else i
+            part = down_rows(y, j, 2)
+            send(part, part, ds.at[2 * i + j], dr.at[y, j], (ctx, x, y_of(s)))
+
     ids = ids_ref[...].astype(F32)
     top = ids.shape[0]
     experts = nz * units
@@ -198,11 +205,6 @@
     @pl.when(is_owner)
     def _():
         meta[turn_own] = routing
-
-    local[2].wait()
-    for i, s in enumerate((1, ny - 1) if ny > 2 else (1,)):
-        py = y_of(s)
-        send(down_rows(y), down_rows(y), ds.at[i], dr.at[y, 0], (ctx, x, py))
 
     for s in range(1, ny):
         py = y_of(s)
@@ -265,36 +267,86 @@
                 place = pl.ds(pl.multiple_of(h * rows + py * own, own), own)
                 arrived(tokens.at[turn_own, place, :], nr.at[py, h])
 
+    local[2].wait()
+    d_send(False)
+    d_send(True)
+
+    tables = {4: ((0, 3, 1, 2), (3, 0, 2, 1)), 2: ((0, 1), (1, 0)), 1: ((0,), (0,))}[turns]
+
     def turn(r, at_y):
         off = lax.rem(z + ny - at_y, ny)
+        near, far = tables[0][r], tables[1][r]
         late = lax.div(2 * off, ny + 1)
-        if turns == 4:
-            near, far = ((0, 3), (3, 0), (1, 2), (2, 1))[r]
-        elif turns == 2:
-            near, far = ((0, 1), (1, 0))[r]
-        else:
-            near, far = 0, 0
         distance = off + ny * (near + (far - near) * late)
         return lax.div(lax.rem(z + nz - distance, nz), ny), distance
 
     my_turns = [turn(r, y) for r in range(turns)]
-
-    def z_step(r, k):
-        t, d = my_turns[r]
+    my_off = lax.rem(z + ny - y, ny)
+
+    def hops_at(off, r):
+        return off + ny * tables[2 * off // (ny + 1)][r]
+
+    def steps_out(off):
+        order = []
+        for r in range(turns):
+            d = hops_at(off, r)
+            order += [(HOP * min(d, nz - d) + k, r, k) for k in range(CHUNKS)]
+        return sorted(order)
+
+    def steps_back(off):
+        order = []
+        for r in range(turns):
+            d = hops_at(off, r)
+            waited = half_ring - d if d <= half_ring else d - half_ring - 1
+            order += [(HOP * waited + k, r, k) for k in range(CHUNKS)]
+        return sorted(order)
+
+    def for_offset(run):
+        for off in range(ny):
+            @pl.when(my_off == off)
+            def _():
+                run(off)
+
+    def z_copies(t, k, way):
         at = pl.ds(k * piece, piece)
-        ref, sem = tokens.at[t, at, :], zr.at[t, k]
-
-        @pl.when(d > 0)
-        def _():
-            arrived(ref, sem)
+        device = (ahead, behind)[way]
+        pair = [remote(tokens.at[t, at, :], tokens.at[t, at, :], zs.at[way, t, k], zr.at[t, k], device)]
+        if k == 0:
+            pair.append(remote(meta.at[t], meta.at[t], ms.at[way, t], mr.at[t], device))
+        return pair
+
+    def z_step(off, r, k):
+        t, d = my_turns[r][0], hops_at(off, r)
+        if d > 0:
+            arrived(tokens.at[t, pl.ds(k * piece, piece), :], zr.at[t, k])
             if k == 0:
                 arrived(meta.at[t], mr.at[t])
-
-        forward, backward = d < half_ring, jnp.logical_or(d == 0, d > half_ring + 1)
-        for way, (go, device) in enumerate(((forward, ahead), (backward, behind))):
-            send(ref, ref, zs.at[way, t, k], sem, device, when=go)
-            if k == 0:
-                send(meta.at[t], meta.at[t], ms.at[way, t], mr.at[t], device, when=go)
+        for way, go in enumerate((d < half_ring, d == 0 or d > half_ring + 1)):
+            if go:
+                for copy in z_copies(t, k, way):
+                    copy.start()
+
+    def z_sent():
+        for r in range(turns):
+            t, d = my_turns[r]
+            for way, go in enumerate((d < half_ring, jnp.logical_or(d == 0, d > half_ring + 1))):
+                @pl.when(go)
+                def _():
+                    for k in range(CHUNKS):
+                        for copy in z_copies(t, k, way):
+                            copy.wait_send()
+
+    def z_part(part):
+        def run(off):
+            order = steps_out(off)
+            ends = [0]
+            for r in range(turns):
+                last = max(i for i, step in enumerate(order) if step[1] == r)
+                ends.append(max(ends[-1], last + 1))
+            for _, r, k in order[ends[part] : ends[part + 1]]:
+                z_step(off, r, k)
+
+        for_offset(run)
 
     slot_row = lax.broadcasted_iota(jnp.int32, (unit, block), 0)
     token_lane = lax.broadcasted_iota(jnp.int32, (unit, block), 1)
@@ -339,42 +391,51 @@
             index, _ = plane_peer(s)
             arrived(gathered.at[y, t, index], xr.at[t, index])
         for i, s in enumerate((1, ny - 1) if ny > 2 else (1,)):
-            send(
-                gathered.at[y, t], gathered.at[y, t], ys.at[i, t], yr.at[y, t, 0],
-                (ctx, x, y_of(s)),
-            )
+            for j in (i, 1 - i):
+                part = gather_half(y, t, j)
+                send(part, part, ys.at[2 * i + j, t], yr.at[y, t, j], (ctx, x, y_of(s)))
+
+    def gather_half(at_y, t, j):
+        return gathered.at[at_y, t, pl.ds(j * (units // 2), units // 2)]
 
     def y_forward(r):
         for i, s in enumerate((ny - 1, 1) if ny > 2 else (1,)):
             py = y_of(s)
             t, _ = turn(r, py)
-            arrived(gathered.at[py, t], yr.at[py, t, 0])
+            part = gather_half(py, t, i)
+            arrived(part, yr.at[py, t, i])
             if ny > 2:
-                part = gathered.at[py, t, pl.ds(i * (units // 2), units // 2)]
-                send(part, part, ys.at[2 + i, t], yr.at[py, t, 1 + i], (ctx, x, y_of(ny - s)))
+                send(part, part, ys.at[4 + i, t], yr.at[py, t, 2 + i], (ctx, x, y_of(ny - s)))
+
+    def y_rest(r):
+        for i, s in enumerate((ny - 1, 1) if ny > 2 else (1,)):
+            py = y_of(s)
+            t, _ = turn(r, py)
+            arrived(gather_half(py, t, 1 - i), yr.at[py, t, 1 - i])
 
     def y_last(r):
         if ny > 2:
             py = y_of(2)
             t, _ = turn(r, py)
             for i in range(2):
-                part = gathered.at[py, t, pl.ds(i * (units // 2), units // 2)]
-                arrived(part, yr.at[py, t, 1 + i])
+                arrived(gather_half(py, t, i), yr.at[py, t, 2 + i])
 
     def d_forward():
         for i, s in enumerate((ny - 1, 1) if ny > 2 else (1,)):
             py = y_of(s)
-            arrived(down_rows(py), dr.at[py, 0])
+            part = down_rows(py, i, 2)
+            arrived(part, dr.at[py, i])
             if ny > 2:
-                part = down_rows(py, i, 2)
-                send(part, part, ds.at[2 + i], dr.at[py, 1 + i], (ctx, x, y_of(ny - s)))
+                send(part, part, ds.at[4 + i], dr.at[py, 2 + i], (ctx, x, y_of(ny - s)))
 
     def d_last():
+        for i, s in enumerate((ny - 1, 1) if ny > 2 else (1,)):
+            py = y_of(s)
+            arrived(down_rows(py, 1 - i, 2), dr.at[py, 1 - i])
         if ny > 2:
             py = y_of(2)
             for i in range(2):
-                part = down_rows(py, i, 2)
-                arrived(part, dr.at[py, 1 + i])
+                arrived(down_rows(py, i, 2), dr.at[py, 2 + i])
 
     def expert(r, s):
         py = y_of(s)
@@ -402,52 +463,52 @@
             )
 
     if turns == 4:
-        for k in range(CHUNKS):
-            z_step(0, k)
-            z_step(1, k)
+        z_part(0)
         pack(0)
+        z_part(1)
+        y_send(0)
         pack(1)
-        for k in range(CHUNKS):
-            z_step(2, k)
-            z_step(3, k)
-            if k == 1:
-                y_send(0)
+        d_forward()
+        z_part(2)
         y_send(1)
+        y_forward(0)
         pack(2)
+        z_part(3)
+        y_send(2)
+        y_forward(1)
         pack(3)
-        d_forward()
-        y_forward(0)
-        y_send(2)
         local[0].wait()
         local[1].wait()
         expert(0, 0)
-        y_forward(1)
+        y_rest(0)
+        expert(0, 1)
         y_send(3)
-        expert(1, 0)
-        expert(0, 1)
         expert(0, 3)
+        y_forward(2)
         y_last(0)
         expert(0, 2)
-        y_forward(2)
+        expert(1, 0)
+        y_rest(1)
         expert(1, 1)
         expert(1, 3)
-        expert(2, 0)
         y_last(1)
         expert(1, 2)
         y_forward(3)
+        expert(2, 0)
         expert(3, 0)
+        y_rest(2)
         expert(2, 1)
         expert(2, 3)
         y_last(2)
         expert(2, 2)
+        y_rest(3)
         expert(3, 1)
         expert(3, 3)
         y_last(3)
         expert(3, 2)
     else:
-        for k in range(CHUNKS):
-            for r in range(turns):
-                z_step(r, k)
+        for r in range(turns):
+            z_part(r)
         for r in range(turns):
             pack(r)
         d_forward()
@@ -458,6 +519,7 @@
         for r in range(turns):
             y_forward(r)
         for r in range(turns):
+            y_rest(r)
             y_last(r)
             for s in range(ny):
                 expert(r, s)
@@ -494,36 +556,46 @@
                 mix[t, 0], data, preferred_element_type=F32
             ) + jnp.dot(mix[t, 1], data, preferred_element_type=F32)
 
-    def z_reduce(r, k):
+    def reduce_copy(r, k):
         t, d = my_turns[r]
         at = pl.ds(k * piece, piece)
         onward = lax.div(d, half_ring + 1)
         next_z = lax.rem(z + nz + 2 * onward - 1, nz)
         slot = t + (turns - t) * lax.div(d, nz - 1)
-        starts = jnp.logical_or(d == half_ring, d == half_ring + 1)
-
-        @pl.when(starts)
-        def _():
-            chain_out[t, at, :] = partial[t, at, :].astype(BF16)
-
-        @pl.when(jnp.logical_not(starts))
-        def _():
+        return remote(
+            chain_out.at[t, at, :], chain_in.at[slot, at, :], qs.at[t, k], qr.at[slot, k],
+            (next_z * nc + c, x, y),
+        )
+
+    def z_reduce(off, r, k):
+        t, d = my_turns[r][0], hops_at(off, r)
+        at = pl.ds(k * piece, piece)
+        total = partial[t, at, :]
+        if d not in (half_ring, half_ring + 1):
             arrived(chain_in.at[t, at, :], qr.at[t, k])
-            total = partial[t, at, :] + chain_in[t, at, :].astype(F32)
-            if r < 2:
-                partial[t, at, :] = total
+            total += chain_in[t, at, :].astype(F32)
+        if d == 0:
+            arrived(chain_in.at[turns, at, :], qr.at[turns, k])
+            total += chain_in[turns, at, :].astype(F32)
+            final[at, :] = total.astype(BF16)
+        else:
             chain_out[t, at, :] = total.astype(BF16)
-
-        send(
-            chain_out.at[t, at, :], chain_in.at[slot, at, :], qs.at[t, k], qr.at[slot, k],
-            (next_z * nc + c, x, y), when=d > 0,
-        )
-        if r < 2:
-            @pl.when(d == 0)
+            reduce_copy(r, k).start()
+
+    def reduce_sent():
+        for r in range(turns):
+            @pl.when(my_turns[r][1] > 0)
             def _():
-                arrived(chain_in.at[turns, at, :], qr.at[turns, k])
-                total = partial[t, at, :] + chain_in[turns, at, :].astype(F32)
-                final[at, :] = total.astype(BF16)
+                for k in range(CHUNKS):
+                    reduce_copy(r, k).wait_send()
+
+    def reduce_part(starting):
+        def run(off):
+            for wait, r, k in steps_back(off):
+                if (wait < CHUNKS and hops_at(off, r) in (half_ring, half_ring + 1)) == starting:
+                    z_reduce(off, r, k)
+
+        for_offset(run)
 
     def hand_out():
         for h in range(2):
@@ -539,23 +611,17 @@
             answer(r)
         combine(3)
         combine(2)
-        for k in range(CHUNKS):
-            z_reduce(3, k)
-            z_reduce(2, k)
-            if k == 0:
-                combine(1)
-                combine(0)
-        for k in range(CHUNKS):
-            z_reduce(1, k)
-            z_reduce(0, k)
+        reduce_part(True)
+        combine(1)
+        combine(0)
+        reduce_part(False)
     else:
         for r in range(turns - 1, -1, -1):
             answer(r)
         for r in range(turns - 1, -1, -1):
             combine(r)
-        for k in range(CHUNKS):
-            for r in range(turns - 1, -1, -1):
-                z_reduce(r, k)
+        reduce_part(True)
+        reduce_part(False)
     hand_out()
 
     @pl.when(is_owner)
@@ -572,6 +638,8 @@
     for h in range(2):
         out_ref[:, pl.ds(h * half, half)] = (state[h] + finished[h].astype(F32)).astype(BF16)
 
+    z_sent()
+    reduce_sent()
     for when, copy in sends:
         if when is None:
             copy.wait_send()
@@ -646,10 +714,10 @@
             sems(4),
             sems(ny), sems(ny), sems(nx), sems(nx), sems(nx), sems(nx), sems(ny), sems(ny),
             sems(2), sems(ny, 2),
-            sems(4), sems(ny, 3),
+            sems(6), sems(ny, 4),
             sems(2, turns, CHUNKS), sems(turns, CHUNKS), sems(2, turns), sems(turns),
             sems(turns, units), sems(turns, units),
-            sems(4, turns), sems(ny, turns, 3),
+            sems(6, turns), sems(ny, turns, 4),
             sems(ny, turns), sems(ny, turns),
             sems(turns, units), sems(turns, units),
             sems(turns, CHUNKS), sems(turns + 1, CHUNKS),

time: 339 us -> 160 us (0.47)
  the two profiles are of different devices: /device:TPU:96 before, /device:TPU:56 now
where the time goes in v3:
time: 160 us
  Pallas kernels  157 us (98%)
  local copies, waits for them, and re-layouts  2.18 us (1%)
    pallas_call x1, Pallas kernels, on_device(): pl.pallas_call(functools.partial(kernel, size), out_shape=jax.ShapeDtypeS...  157 us

profile of v3, /device:TPU:56, one launch (start us, length us, event | category | flops | bytes accessed | tf_op | source)
XLA Modules:
  0.0 160.2 jit_solution(2540847803162225031)
XLA Ops:
  0.0 0.0 copy-start
  0.0 0.7 copy-done
  0.7 0.0 copy-start.1
  0.7 0.7 pad_add_fusion.ids_ref
  1.4 0.0 copy-done.1
  1.4 0.7 pad_maximum_fusion.choice_ref
  2.0 156.6 %shard_map.91 = bf16[16,2048]{1,0:T(8,128)(2,1)} custom-call(bf16[256,256]{1,0:T(8,128)(2,1)} %attn_ref.1, bf16[256,2048]{1,0:T(8,128)(2,1)} %weight_ref.1, bf16[64,2048]{1,0:T(8,128)(2,1)} %residual_ref.1, f32[1,2048]{1,0:T(1,128)} %bitcast.9, s32[8,128]{1,0:T(8,128)} %pad_add_fusion.ids_ref, f32[8,128]{1,0:T(8,128)} %pad_maximum_fusion.choice_ref, ...), custom_call_target="tpu_custom_call" | custom-call | tf_op jit(solution)/shard_map/pallas_call | solution.py:681
  158.7 1.5 copy.11
Async XLA Ops:
  0.0 0.7 copy-start
  0.7 0.7 copy-start.1

commit v4 on v3

--- a/solution.py
+++ b/solution.py
@@ -167,6 +167,7 @@
             send(part, part, ds.at[2 * i + j], dr.at[y, j], (ctx, x, y_of(s)))
 
     ids = ids_ref[...].astype(F32)
+    ids = jnp.concatenate([ids, ids], axis=1)
     top = ids.shape[0]
     experts = nz * units
     expert_row = lax.broadcasted_iota(jnp.int32, (experts, block), 0).astype(F32)
@@ -194,7 +195,7 @@
         ],
         axis=0,
     )
-    choice = choice_ref[...]
+    choice = jnp.concatenate([choice_ref[...], choice_ref[...]], axis=1)
     probs = choice / jnp.sum(choice, axis=0, keepdims=True)
     high = probs.astype(BF16).astype(F32)
     turn_own = lax.div(z, ny)
@@ -353,27 +354,32 @@
     same_half = lax.div(slot_row, CAP) == lax.div(token_lane, rows)
     slot_want = jnp.where(same_half, lax.rem(slot_row, CAP), -2).astype(F32)
 
+    def routed_here(t, values):
+        table = meta[t].astype(F32)
+        first = (z * units).astype(F32)
+        found = [[] for _ in range(1 + values)]
+        for u in range(units):
+            got = [jnp.full((unit, block), -1.0, F32)]
+            got += [jnp.zeros((unit, block), F32)] * values
+            for k in range(top):
+                hit = table[k : k + 1] == first + float(u)
+                for i in range(1 + values):
+                    row = (1 + i) * top + k
+                    got[i] = jnp.where(hit, table[row : row + 1], got[i])
+            hit = got[0] == slot_want
+            for i in range(1 + values):
+                found[i].append(jnp.where(hit, 1.0 if i == 0 else got[i], 0.0))
+        return [jnp.concatenate(parts, axis=0) for parts in found]
+
+    def weigh(r):
+        t, _ = my_turns[r]
+        _, big, small = routed_here(t, 2)
+        mix[t, 0] = big.T.astype(BF16)
+        mix[t, 1] = small.T.astype(BF16)
+
     def pack(r):
         t, _ = my_turns[r]
-        table = meta[t].astype(F32)
-        first = (z * units).astype(F32)
-        picks, highs, lows = [], [], []
-        for u in range(units):
-            got = jnp.full((unit, block), -1.0, F32)
-            big = jnp.zeros((unit, block), F32)
-            small = jnp.zeros((unit, block), F32)
-            for k in range(top):
-                hit = table[k : k + 1] == first + float(u)
-                got = jnp.where(hit, table[top + k : top + k + 1], got)
-                big = jnp.where(hit, table[2 * top + k : 2 * top + k + 1], big)
-                small = jnp.where(hit, table[3 * top + k : 3 * top + k + 1], small)
-            hit = got == slot_want
-            picks.append(jnp.where(hit, 1.0, 0.0))
-            highs.append(jnp.where(hit, big, 0.0))
-            lows.append(jnp.where(hit, small, 0.0))
-        chosen = jnp.concatenate(picks, axis=0).astype(BF16)
-        mix[t, 0] = jnp.concatenate(highs, axis=0).T.astype(BF16)
-        mix[t, 1] = jnp.concatenate(lows, axis=0).T.astype(BF16)
+        chosen = routed_here(t, 0)[0].astype(BF16)
         for j in range(2):
             at = pl.ds(j * cols, cols)
             out = jnp.dot(chosen, tokens[t, :, at], preferred_element_type=F32)
@@ -468,7 +474,6 @@
         z_part(1)
         y_send(0)
         pack(1)
-        d_forward()
         z_part(2)
         y_send(1)
         y_forward(0)
@@ -480,9 +485,12 @@
         local[0].wait()
         local[1].wait()
         expert(0, 0)
+        weigh(3)
+        weigh(2)
         y_rest(0)
         expert(0, 1)
         y_send(3)
+        d_forward()
         expert(0, 3)
         y_forward(2)
         y_last(0)
@@ -494,6 +502,8 @@
         y_last(1)
         expert(1, 2)
         y_forward(3)
+        weigh(1)
+        weigh(0)
         expert(2, 0)
         expert(3, 0)
         y_rest(2)
@@ -511,6 +521,7 @@
             z_part(r)
         for r in range(turns):
             pack(r)
+            weigh(r)
         d_forward()
         local[0].wait()
         local[1].wait()
@@ -578,6 +589,12 @@
             arrived(chain_in.at[turns, at, :], qr.at[turns, k])
             total += chain_in[turns, at, :].astype(F32)
             final[at, :] = total.astype(BF16)
+            for row in range(k * piece, (k + 1) * piece, own):
+                h, py = row // rows, row % rows // own
+
+                @pl.when(y != py)
+                def _():
+                    hand_copy(h, py).start()
         else:
             chain_out[t, at, :] = total.astype(BF16)
             reduce_copy(r, k).start()
@@ -589,40 +606,45 @@
                 for k in range(CHUNKS):
                     reduce_copy(r, k).wait_send()
 
-    def reduce_part(starting):
+    def reduce_part(part):
         def run(off):
             for wait, r, k in steps_back(off):
-                if (wait < CHUNKS and hops_at(off, r) in (half_ring, half_ring + 1)) == starting:
+                begins = hops_at(off, r) in (half_ring, half_ring + 1)
+                if part == (0 if begins else 1 if turns == 4 and wait < 2 * HOP + 1 and r > 1 else 2):
                     z_reduce(off, r, k)
 
         for_offset(run)
 
-    def hand_out():
-        for h in range(2):
-            for py in range(ny):
-                place = pl.ds(h * rows + py * own, own)
-                send(
-                    final.at[place, :], finished.at[h], fs.at[h, py], fr.at[h], (ctx, x, py),
-                    when=jnp.logical_and(is_owner, y != py),
-                )
+    def hand_copy(h, py):
+        place = pl.ds(h * rows + py * own, own)
+        return remote(final.at[place, :], finished.at[h], fs.at[h, py], fr.at[h], (ctx, x, py))
+
+    def handed_out():
+        for py in range(ny):
+            @pl.when(jnp.logical_and(is_owner, y != py))
+            def _():
+                for h in range(2):
+                    hand_copy(h, py).wait_send()
 
     if turns == 4:
-        for r in (3, 2, 1, 0):
-            answer(r)
+        answer(3)
+        answer(2)
         combine(3)
+        reduce_part(0)
         combine(2)
-        reduce_part(True)
+        answer(1)
+        answer(0)
+        reduce_part(1)
         combine(1)
         combine(0)
-        reduce_part(False)
+        reduce_part(2)
     else:
         for r in range(turns - 1, -1, -1):
             answer(r)
         for r in range(turns - 1, -1, -1):
             combine(r)
-        reduce_part(True)
-        reduce_part(False)
-    hand_out()
+        reduce_part(0)
+        reduce_part(2)
 
     @pl.when(is_owner)
     def _():
@@ -640,6 +662,7 @@
 
     z_sent()
     reduce_sent()
+    handed_out()
     for when, copy in sends:
         if when is None:
             copy.wait_send()
@@ -667,8 +690,7 @@
     share = gate_weight.shape[1]
     top = routed_experts.shape[1]
     units, turns, unit, block = nc * nx, nz // ny, 2 * CAP, 2 * rows
-    ids = jnp.concatenate([routed_experts.T, routed_experts.T], axis=1)
-    choice = jnp.concatenate([route_weights.T, route_weights.T], axis=1)
+    ids, choice = routed_experts.T, route_weights.T
 
     def vmem(*shape, dtype=BF16):
         return pltpu.VMEM(shape, dtype)

time: 160 us -> 156 us (0.975)
  the two profiles are of different devices: /device:TPU:56 before, /device:TPU:64 now
where the time goes in v4:
time: 156 us
  Pallas kernels  155 us (99%)
    pallas_call x1, Pallas kernels, on_device(): pl.pallas_call(functools.partial(kernel, size), out_shape=jax.ShapeDtypeS...  155 us

profile of v4, /device:TPU:64, one launch (start us, length us, event | category | flops | bytes accessed | tf_op | source)
XLA Modules:
  0.0 156.0 jit_solution(11525757535704178534)
XLA Ops:
  0.0 154.5 %shard_map.91 = bf16[16,2048]{1,0:T(8,128)(2,1)} custom-call(bf16[256,256]{1,0:T(8,128)(2,1)} %attn_ref.1, bf16[256,2048]{1,0:T(8,128)(2,1)} %weight_ref.1, bf16[64,2048]{1,0:T(8,128)(2,1)} %residual_ref.1, f32[1,2048]{1,0:T(1,128)} %bitcast.9, s32[8,64]{1,0:T(8,128)} %bitcast.10, f32[8,64]{1,0:T(8,128)} %bitcast.11, bf16[256,2048]{1,0:T(8,128)(2,1)} %bitcast.6, ...), custom_call_target="tpu_custom_call" | custom-call | tf_op jit(solution)/shard_map/pallas_call | solution.py:703
  154.5 1.5 copy.11
